TPU v7x, 256 devices: a whole 4x4x8 slice. The times are simulated.
256 devices in a mesh: section: 8 (over y, core), expert: 32 (over z, x).
Axes of the slice: x: 4, y: 4, z: 8, core: 2. Of those that a mesh axis runs over, the one named last changes fastest.
Arguments:
- tokens: bfloat16 [4096, 7168], P('expert', 'section'), may hold values from -6 to 6
- routes: int32 [4096, 8], P('expert'), may hold values from 0 to 63, all different within a row; in each aligned block of 128 rows (0 to 127, 128 to 255, ...) at most 24 rows name the same one
- combine: float32 [4096, 8], P('expert'), may hold values from 0.05 to 0.6
- gate_weight: bfloat16 [64, 7168, 1024], P('expert', 'section'), may hold values from -0.0625 to 0.0625
- up_weight: bfloat16 [64, 7168, 1024], P('expert', 'section'), may hold values from -0.0625 to 0.0625
- down_weight: bfloat16 [64, 1024, 7168], P('expert', None, 'section'), may hold values from -0.1875 to 0.1875
Outputs:
- mixed: bfloat16 [4096, 7168], P('expert', 'section')
Inputs may be any that keep to these rules, and one draw needn't show every extreme that they name: `routes`: among the 128 rows of one block of tokens, no expert is named more than 24 times; in every draw some expert is named exactly 24 times in some block. The 8 experts of a token differ.
All inputs are finite; a program needn't handle non-finite values.
Results may differ from a plain program's by a relative error of at most 0.029.
Values may be sent and summed in bfloat16 or wider, within the bound.
No kernel may reach another device: no remote copies, remote signals or barrier semaphores. Data moves between devices by JAX's collectives and lax.ppermute only.
A program may use at most 64 MiB of HBM per device.

v0:
```python
import jax
import jax.numpy as jnp
from jax import lax
from jax.sharding import PartitionSpec as P


def body(tokens, routes, combine, gate_weight, up_weight, down_weight):
    groups = lax.axis_size("expert")
    per_device = gate_weight.shape[0]
    experts_all = per_device * groups
    tok_rows, feat_width = tokens.shape
    fanout = routes.shape[1]
    capacity = 3 * tok_rows * fanout // (2 * experts_all)
    flat_routes = routes.reshape(-1)
    onehot = (flat_routes[:, None] == jnp.arange(experts_all, dtype=jnp.int32)[None, :]).astype(
        jnp.int32
    )
    slot_index = jnp.sum(jnp.cumsum(onehot, axis=0) * onehot, axis=1) - 1
    owner_row = jnp.arange(flat_routes.shape[0], dtype=jnp.int32) // fanout
    outbox = jnp.zeros((experts_all, capacity, feat_width), jnp.bfloat16)
    outbox = outbox.at[flat_routes, slot_index].set(tokens[owner_row])
    outbox = outbox.reshape(groups, per_device, capacity, feat_width)
    arrived = lax.all_to_all(outbox, "expert", split_axis=0, concat_axis=0, tiled=True)
    gate_part = jnp.einsum(
        "secd,edf->secf", arrived, gate_weight, preferred_element_type=jnp.float32
    )
    up_part = jnp.einsum("secd,edf->secf", arrived, up_weight, preferred_element_type=jnp.float32)
    gate_sum, up_sum = (
        lax.psum(gate_part.astype(jnp.bfloat16), "section").astype(jnp.float32),
        lax.psum(up_part.astype(jnp.bfloat16), "section").astype(jnp.float32),
    )
    hidden = (jax.nn.silu(gate_sum) * up_sum).astype(jnp.bfloat16)
    result = jnp.einsum("secf,efd->secd", hidden, down_weight, preferred_element_type=jnp.float32)
    returned = lax.all_to_all(
        result.astype(jnp.bfloat16), "expert", split_axis=0, concat_axis=0, tiled=True
    )
    table = returned.reshape(experts_all * capacity, feat_width)
    gathered = table[flat_routes * capacity + slot_index].astype(jnp.float32)
    mixed = jnp.sum(gathered.reshape(tok_rows, fanout, feat_width) * combine[:, :, None], axis=1)
    return mixed.astype(jnp.bfloat16)


def solution(mesh):
    return jax.shard_map(
        body,
        mesh=mesh,
        in_specs=(
            P("expert", "section"),
            P("expert", None),
            P("expert", None),
            P("expert", "section", None),
            P("expert", "section", None),
            P("expert", None, "section"),
        ),
        out_specs=P("expert", "section"),
        check_vma=False,
    )
```

profile of v0, /device:TPU:15, one launch (start us, length us, event | category | flops | bytes accessed | tf_op | source)
XLA Modules:
  0.0 313.8 jit_solution(402005851895858947)
XLA Ops:
  6.5 0.8 copy.16
  7.4 0.1 eq.29
  7.5 0.1 eq.25
  7.6 0.1 reshape.148
  7.7 18.0 %reduce-window.6 = s32[64,8,128]{2,1,0:T(8,128)S(1)} reduce-window(s32[64,8,128]{2,1,0:T(8,128)S(1)} %fusion.32, s32[]{:T(128)} %constant.31.clone.1), window={size=1x1x128 pad=0_0x0_0x127_0}, to_apply=%region_0.0 | reduce-window | flops 8323072 | bytes 524292 | tf_op jit(solution)/shard_map/reduce-window
  25.7 0.1 slice.12
  25.8 0.1 copy.19
  26.0 0.1 copy.20
  26.1 0.1 broadcast_add_fusion
  26.3 0.1 fusion.31
  26.4 0.7 multiply_reduce_fusion
  27.1 0.7 and_reduce_fusion
  27.9 13.0 %scatter_custom_fusion = bf16[1536,896]{1,0:T(8,128)(2,1)S(1)} fusion(s32[1024]{0:T(1024)S(1)} %get-tuple-element.13, bf16[128,896]{1,0:T(8,128)(2,1)S(1)} %copy-done, s32[1024]{0:T(1024)S(1)} %get-tuple-element.12, bf16[]{:T(256)} %constant.30.clone.1), kind=kCustom, calls=%fused_computation.23 | custom fusion | bytes 2752514
  40.9 74.7 %all_to_all.10 = bf16[32,2,24,896]{3,2,1,0:T(8,128)(2,1)S(1)} all-to-all(bf16[32,2,24,896]{3,2,1,0:T(8,128)(2,1)S(1)} %bitcast.51), channel_id=1, replica_groups=mesh['section'=8,'expert'=32] {'expert'}, dimensions={0} | all-to-all | bytes 5505024 | tf_op jit(solution)/shard_map/all_to_all | solution.py:23
  115.5 4.9 %convert_bitcast_fusion = bf16[32,2,24,1024]{3,2,0,1:T(8,128)(2,1)} fusion(bf16[2,896,1024]{2,1,0:T(8,128)(2,1)S(1)} %copy-done.2, bf16[32,2,24,896]{3,2,1,0:T(8,128)(2,1)S(1)} %all_to_all.10), kind=kOutput, calls=%fused_computation.18 | convolution fusion | flops 2820145152 | bytes 9568256 | tf_op jit(solution)/shard_map/secd,edf->secf/dot_general | solution.py:27
  120.4 4.8 %convert_bitcast_fusion.1 = bf16[32,2,24,1024]{3,2,0,1:T(8,128)(2,1)} fusion(bf16[2,896,1024]{2,1,0:T(8,128)(2,1)S(1)} %copy-done.3, bf16[32,2,24,896]{3,2,1,0:T(8,128)(2,1)S(1)} %all_to_all.10), kind=kOutput, calls=%fused_computation.19 | convolution fusion | flops 2820145152 | bytes 9568256 | tf_op jit(solution)/shard_map/secd,edf->secf/dot_general | solution.py:24
  125.2 87.4 %all-reduce.3.cloned.1.call-done = (bf16[32,2,24,1024]{3,2,0,1:T(8,128)(2,1)}, bf16[32,2,24,1024]{3,2,0,1:T(8,128)(2,1)}) async-done(((bf16[32,2,24,1024]{3,2,0,1:T(8,128)(2,1)}, bf16[32,2,24,1024]{3,2,0,1:T(8,128)(2,1)}), (bf16[32,2,24,1024]{3,2,0,1:T(8,128)(2,1)}, bf16[32,2,24,1024]{3,2,0,1:T(8,128)(2,1)})) %all-reduce.3.cloned.1.call-update) | async-done | bytes 6291472 | tf_op jit(solution)/shard_map/psum | solution.py:30
  212.6 8.1 %convert_bitcast_fusion.2 = bf16[32,2,24,896]{3,2,0,1:T(8,128)(2,1)S(1)} fusion(bf16[2,1024,896]{2,1,0:T(8,128)(2,1)} %param.11, bf16[32,2,24,1024]{3,2,0,1:T(8,128)(2,1)} %get-tuple-element.5, bf16[32,2,24,1024]{3,2,0,1:T(8,128)(2,1)} %get-tuple-element.6), kind=kOutput, calls=%fused_computation.20 | convolution fusion | flops 2832531456 | bytes 12713984 | tf_op jit(solution)/shard_map/secf,efd->secd/dot_general | solution.py:33
  220.7 1.8 copy.23
  222.4 9.7 %all-to-all-start.1 = ((bf16[32,2,24,896]{3,2,1,0:T(8,128)(2,1)}), bf16[32,2,24,896]{3,2,1,0:T(8,128)(2,1)S(1)}, u32[]{:S(2)}, u32[]{:S(2)}) async-start(bf16[32,2,24,896]{3,2,1,0:T(8,128)(2,1)} %copy.23), calls=%async_computation.1 | async-start | bytes 5505024 | tf_op jit(solution)/shard_map/all_to_all | solution.py:34
  232.2 0.1 copy.24
  232.3 66.1 %all-to-all-done.1 = bf16[32,2,24,896]{3,2,1,0:T(8,128)(2,1)S(1)} async-done(((bf16[32,2,24,896]{3,2,1,0:T(8,128)(2,1)}), bf16[32,2,24,896]{3,2,1,0:T(8,128)(2,1)S(1)}, u32[]{:S(2)}, u32[]{:S(2)}) %all-to-all-start.1) | async-done | bytes 2752544 | tf_op jit(solution)/shard_map/all_to_all | solution.py:34
  298.3 5.2 %gather_fusion = bf16[1024,896]{1,0:T(8,128)(2,1)} fusion(bf16[1536,896]{1,0:T(8,128)(2,1)S(1)} %bitcast.50, s32[1024]{0:T(1024)S(1)} %broadcast_clamp_fusion), kind=kCustom, calls=%fused_computation.1 | custom fusion | bytes 3674112 | tf_op jit(solution)/shard_map/gather | solution.py:38
  303.6 3.4 %fusion.5 = bf16[128,896]{1,0:T(8,128)(2,1)} fusion(bf16[1024,896]{1,0:T(8,128)(2,1)} %gather_fusion, f32[128,8]{1,0:T(8,128)S(1)} %copy.24), kind=kLoop, calls=%fused_computation.11 | loop fusion | flops 2637824 | bytes 2068480 | tf_op jit(solution)/shard_map/reduce_sum | solution.py:39
  (18 shorter events, 0.1 us)
Async XLA Ops:
  6.5 21.3 %copy-start = (bf16[128,896]{1,0:T(8,128)(2,1)S(1)}, bf16[128,896]{1,0:T(8,128)(2,1)}, u32[]{:S(2)}) copy-start(bf16[128,896]{1,0:T(8,128)(2,1)} %param.6) | copy-start | bytes 688132
  6.5 206.1 %all-reduce.3.cloned.1.call-start = ((), (), s32[]{:S(2)}) async-start(), calls=%async_computation.2 | async-start | bytes 12582912 | tf_op jit(solution)/shard_map/psum | solution.py:30
  40.8 74.7 %copy-start.2 = (bf16[2,896,1024]{2,1,0:T(8,128)(2,1)S(1)}, bf16[2,896,1024]{2,1,0:T(8,128)(2,1)}, u32[]{:S(2)}) copy-start(bf16[2,896,1024]{2,1,0:T(8,128)(2,1)} %param.10) | copy-start | bytes 11010052
  115.5 4.9 %copy-start.3 = (bf16[2,896,1024]{2,1,0:T(8,128)(2,1)S(1)}, bf16[2,896,1024]{2,1,0:T(8,128)(2,1)}, u32[]{:S(2)}) copy-start(bf16[2,896,1024]{2,1,0:T(8,128)(2,1)} %param.9) | copy-start | bytes 11010052
  222.4 9.7 %copy-start.1 = (f32[128,8]{0,1:T(8,128)S(1)}, f32[128,8]{0,1:T(8,128)}, u32[]{:S(2)}) copy-start(f32[128,8]{0,1:T(8,128)} %param.8) | copy-start | bytes 12292
  222.4 75.9 %all-to-all-start.1 = ((bf16[32,2,24,896]{3,2,1,0:T(8,128)(2,1)}), bf16[32,2,24,896]{3,2,1,0:T(8,128)(2,1)S(1)}, u32[]{:S(2)}, u32[]{:S(2)}) async-start(bf16[32,2,24,896]{3,2,1,0:T(8,128)(2,1)} %copy.23), calls=%async_computation.1 | async-start | bytes 5505024 | tf_op jit(solution)/shard_map/all_to_all | solution.py:34
Sparse Core Ops, SparseCore 0:
  125.4 87.1 all-reduce.2
where the time goes:
time: 314 us
  waiting for transfers between devices  153 us (49%)
  blocking collectives  74.7 us (24%)
  other arithmetic  23.2 us (7%)
  local copies, waits for them, and re-layouts  21.6 us (7%)
  matrix products  17.7 us (6%)
  between operations  13.5 us (4%)
  starting transfers between devices  9.7 us (3%)
    psum x1, waiting for transfers between devices, body(): lax.psum(up_part.astype(jnp.bfloat16), 'section').astype(jnp.float32)  87.4 us
    all_to_all x1, blocking collectives, body(): lax.all_to_all(outbox, 'expert', split_axis=0, concat_axis=0, tiled=True)  74.7 us
    all_to_all x1, waiting for transfers between devices, body(): lax.all_to_all(result.astype(jnp.bfloat16), 'expert', split_axis=0, conca...  66.1 us
    another operation x3, other arithmetic  18.2 us
    unnamed x11, local copies, waits for them, and re-layouts  13.9 us
    all_to_all x1, starting transfers between devices, body(): lax.all_to_all(result.astype(jnp.bfloat16), 'expert', split_axis=0, conca...  9.7 us
    dot_general x1, matrix products, body(): jnp.einsum('secf,efd->secd', hidden, down_weight, preferred_element_type=...  8.06 us
  transfers between devices with their start and end apart: 2, of which 2 were waited for; matrix products, arithmetic and copies ran while one was open for 0% of the time, Pallas kernels for 0%

commit v1 on v0

--- a/solution.py
+++ b/solution.py
@@ -27,7 +27,9 @@
     up_part = jnp.einsum("secd,edf->secf", arrived, up_weight, preferred_element_type=jnp.float32)
     gate_sum, up_sum = (
         lax.psum(gate_part.astype(jnp.bfloat16), "section").astype(jnp.float32),
-        lax.psum(up_part.astype(jnp.bfloat16), "section").astype(jnp.float32),
+        jnp.sum(lax.all_gather(up_part.astype(jnp.bfloat16), "section"), axis=0).astype(
+            jnp.float32
+        ),
     )
     hidden = (jax.nn.silu(gate_sum) * up_sum).astype(jnp.bfloat16)
     result = jnp.einsum("secf,efd->secd", hidden, down_weight, preferred_element_type=jnp.float32)

time: 314 us -> 420 us (1.34); the launches traced: 314 us -> 415 us
  waiting for transfers between devices: 153 us -> 236 us
  other arithmetic: 23.2 us -> 37.4 us
    all_gather x0 -> x1, waiting for transfers between devices: none -> 113 us  [body(): lax.all_gather(up_part.astype(jnp.bfloat16), 'section')]
    psum x1, waiting for transfers between devices: 87.4 us -> 59.5 us  [body(): lax.psum(gate_part.astype(jnp.bfloat16), 'section').astype(jnp.float32)]
    reduce_sum x0 -> x1, other arithmetic: none -> 14.2 us  [body(): jnp.sum(lax.all_gather(up_part.astype(jnp.bfloat16), 'section'), axis=0)]
    unnamed x11 -> x13, local copies, waits for them, and re-layouts: 13.9 us -> 17.1 us
  transfers between devices with their start and end apart: 2 -> 3, of which waited for: 2 -> 3; matrix products, arithmetic and copies ran while one was open for 0% -> 5% of each run, Pallas kernels for 0% -> 0%
where the time goes in v1:
time: 420 us; the launch traced here: 415 us
  waiting for transfers between devices  236 us (56%)
  blocking collectives  74.7 us (18%)
  other arithmetic  37.4 us (9%)
  local copies, waits for them, and re-layouts  24.7 us (6%)
  matrix products  18.9 us (4%)
  between operations  13.5 us (3%)
  starting transfers between devices  9.93 us (2%)
    all_gather x1, waiting for transfers between devices, body(): lax.all_gather(up_part.astype(jnp.bfloat16), 'section')  113 us
    all_to_all x1, blocking collectives, body(): lax.all_to_all(outbox, 'expert', split_axis=0, concat_axis=0, tiled=True)  74.7 us
    all_to_all x1, waiting for transfers between devices, body(): lax.all_to_all(result.astype(jnp.bfloat16), 'expert', split_axis=0, conca...  63.6 us
    psum x1, waiting for transfers between devices, body(): lax.psum(gate_part.astype(jnp.bfloat16), 'section').astype(jnp.float32)  59.5 us
    another operation x3, other arithmetic  18.2 us
    unnamed x13, local copies, waits for them, and re-layouts  17.1 us
    reduce_sum x1, other arithmetic, body(): jnp.sum(lax.all_gather(up_part.astype(jnp.bfloat16), 'section'), axis=0)  14.2 us
    all_to_all x1, starting transfers between devices, body(): lax.all_to_all(result.astype(jnp.bfloat16), 'expert', split_axis=0, conca...  9.7 us
  transfers between devices with their start and end apart: 3, of which 3 were waited for; matrix products, arithmetic and copies ran while one was open for 5% of the time, Pallas kernels for 0%

profile of v1, /device:TPU:15, one launch (start us, length us, event | category | flops | bytes accessed | tf_op | source)
XLA Modules:
  0.0 415.4 jit_solution(11053549387069149831)
XLA Ops:
  6.5 0.8 copy.16
  7.7 18.0 %reduce-window.6 = s32[64,8,128]{2,1,0:T(8,128)S(1)} reduce-window(s32[64,8,128]{2,1,0:T(8,128)S(1)} %fusion.32, s32[]{:T(128)} %constant.32.clone.1), window={size=1x1x128 pad=0_0x0_0x127_0}, to_apply=%region_0.0 | reduce-window | flops 8323072 | bytes 524292 | tf_op jit(solution)/shard_map/reduce-window
  25.7 0.1 slice.12
  25.8 0.1 copy.19
  26.1 0.1 broadcast_add_fusion
  26.4 0.7 multiply_reduce_fusion
  27.1 0.7 and_reduce_fusion
  27.9 13.0 %scatter_custom_fusion = bf16[1536,896]{1,0:T(8,128)(2,1)S(1)} fusion(s32[1024]{0:T(1024)S(1)} %get-tuple-element.11, bf16[128,896]{1,0:T(8,128)(2,1)S(1)} %copy-done, s32[1024]{0:T(1024)S(1)} %get-tuple-element.10, bf16[]{:T(256)} %constant.31.clone.1), kind=kCustom, calls=%fused_computation.23 | custom fusion | bytes 2752514
  40.9 74.7 %all_to_all.10 = bf16[32,2,24,896]{3,2,1,0:T(8,128)(2,1)S(1)} all-to-all(bf16[32,2,24,896]{3,2,1,0:T(8,128)(2,1)S(1)} %bitcast.53), channel_id=1, replica_groups=mesh['section'=8,'expert'=32] {'expert'}, dimensions={0} | all-to-all | bytes 5505024 | tf_op jit(solution)/shard_map/all_to_all | solution.py:23
  115.5 1.6 copy-done.1
  117.2 4.8 %convert_bitcast_fusion = bf16[32,2,24,1024]{3,2,0,1:T(8,128)(2,1)} fusion(bf16[2,896,1024]{2,1,0:T(8,128)(2,1)S(1)} %copy-done.4, bf16[32,2,24,896]{3,2,1,0:T(8,128)(2,1)S(1)} %all_to_all.10), kind=kOutput, calls=%fused_computation.18 | convolution fusion | flops 2820145152 | bytes 9568256 | tf_op jit(solution)/shard_map/secd,edf->secf/dot_general | solution.py:27
  122.0 0.2 all-reduce.2.cloned.1.call-start
  122.2 1.5 copy-done.2
  123.7 6.9 %convert_bitcast_fusion.1 = bf16[32,2,24,1024]{3,2,0,1:T(8,128)(2,1)} fusion(bf16[2,896,1024]{2,1,0:T(8,128)(2,1)} %param.9, bf16[32,2,24,896]{3,2,1,0:T(8,128)(2,1)S(1)} %copy-done.2), kind=kOutput, calls=%fused_computation.19 | convolution fusion | flops 2820145152 | bytes 9568256 | tf_op jit(solution)/shard_map/secd,edf->secf/dot_general | solution.py:24
  130.6 113.1 %all-gather.3.cloned.1.call-done = bf16[256,2,24,1024]{3,2,0,1:T(8,128)(2,1)} async-done(((bf16[32,2,24,1024]{3,2,0,1:T(8,128)(2,1)}), bf16[256,2,24,1024]{3,2,0,1:T(8,128)(2,1)}) %all-gather.3.cloned.1.call-update) | async-done | bytes 25165840 | tf_op jit(solution)/shard_map/all_gather | solution.py:30
  243.7 14.2 %reduce_sum.31 = bf16[32,2,24,1024]{3,2,0,1:T(8,128)(2,1)S(1)} reduce(bf16[8,32,2,24,1024]{4,3,1,0,2:T(8,128)(2,1)} %bitcast.52, bf16[]{:T(256)} %constant.31.clone.1), dimensions={0}, to_apply=%region_5.6 | reduce | flops 11010048 | bytes 28311554 | tf_op jit(solution)/shard_map/reduce_sum | solution.py:30
  257.9 59.5 %all-reduce.2.cloned.1.call-done = bf16[32,2,24,1024]{3,2,0,1:T(8,128)(2,1)} async-done(((bf16[32,2,24,1024]{3,2,0,1:T(8,128)(2,1)}), bf16[32,2,24,1024]{3,2,0,1:T(8,128)(2,1)}) %all-reduce.2.cloned.1.call-update) | async-done | bytes 3145744 | tf_op jit(solution)/shard_map/psum | solution.py:29
  317.5 7.2 %convert_bitcast_fusion.2 = bf16[32,2,24,896]{3,2,0,1:T(8,128)(2,1)S(1)} fusion(bf16[2,1024,896]{2,1,0:T(8,128)(2,1)} %param.11, bf16[32,2,24,1024]{3,2,0,1:T(8,128)(2,1)S(1)} %reduce_sum.31, bf16[32,2,24,1024]{3,2,0,1:T(8,128)(2,1)} %all-reduce.2.cloned.1.call-done), kind=kOutput, calls=%fused_computation.20 | convolution fusion | flops 2832531456 | bytes 12713984 | tf_op jit(solution)/shard_map/secf,efd->secd/dot_general | solution.py:35
  324.7 1.8 copy.23
  326.5 9.7 %all-to-all-start.1 = ((bf16[32,2,24,896]{3,2,1,0:T(8,128)(2,1)}), bf16[32,2,24,896]{3,2,1,0:T(8,128)(2,1)S(1)}, u32[]{:S(2)}, u32[]{:S(2)}) async-start(bf16[32,2,24,896]{3,2,1,0:T(8,128)(2,1)} %copy.23), calls=%async_computation.1 | async-start | bytes 5505024 | tf_op jit(solution)/shard_map/all_to_all | solution.py:36
  336.2 0.1 copy.24
  336.3 63.6 %all-to-all-done.1 = bf16[32,2,24,896]{3,2,1,0:T(8,128)(2,1)S(1)} async-done(((bf16[32,2,24,896]{3,2,1,0:T(8,128)(2,1)}), bf16[32,2,24,896]{3,2,1,0:T(8,128)(2,1)S(1)}, u32[]{:S(2)}, u32[]{:S(2)}) %all-to-all-start.1) | async-done | bytes 2752544 | tf_op jit(solution)/shard_map/all_to_all | solution.py:36
  400.0 5.2 %gather_fusion = bf16[1024,896]{1,0:T(8,128)(2,1)} fusion(bf16[1536,896]{1,0:T(8,128)(2,1)S(1)} %bitcast.51, s32[1024]{0:T(1024)S(1)} %broadcast_clamp_fusion), kind=kCustom, calls=%fused_computation.1 | custom fusion | bytes 3674112 | tf_op jit(solution)/shard_map/gather | solution.py:40
  405.2 3.4 fusion.5
  (24 shorter events, 0.6 us)
Async XLA Ops:
  6.5 21.3 %copy-start = (bf16[128,896]{1,0:T(8,128)(2,1)S(1)}, bf16[128,896]{1,0:T(8,128)(2,1)}, u32[]{:S(2)}) copy-start(bf16[128,896]{1,0:T(8,128)(2,1)} %param.6) | copy-start | bytes 688132
  6.5 237.2 %all-gather.3.cloned.1.call-start = ((), (), s32[]{:S(2)}) async-start(), calls=%async_computation.3 | async-start | bytes 28311552 | tf_op jit(solution)/shard_map/all_gather | solution.py:30
  40.8 76.3 %copy-start.4 = (bf16[2,896,1024]{2,1,0:T(8,128)(2,1)S(1)}, bf16[2,896,1024]{2,1,0:T(8,128)(2,1)}, u32[]{:S(2)}) copy-start(bf16[2,896,1024]{2,1,0:T(8,128)(2,1)} %param.10) | copy-start | bytes 11010052
  115.5 1.6 copy-start.1
  122.0 1.8 copy-start.2
  122.0 195.5 %all-reduce.2.cloned.1.call-start = ((), (), s32[]{:S(2)}) async-start(), calls=%async_computation.2 | async-start | bytes 6291456 | tf_op jit(solution)/shard_map/psum | solution.py:29
  326.5 9.7 %copy-start.3 = (f32[128,8]{0,1:T(8,128)S(1)}, f32[128,8]{0,1:T(8,128)}, u32[]{:S(2)}) copy-start(f32[128,8]{0,1:T(8,128)} %param.8) | copy-start | bytes 12292
  326.5 73.5 %all-to-all-start.1 = ((bf16[32,2,24,896]{3,2,1,0:T(8,128)(2,1)}), bf16[32,2,24,896]{3,2,1,0:T(8,128)(2,1)S(1)}, u32[]{:S(2)}, u32[]{:S(2)}) async-start(bf16[32,2,24,896]{3,2,1,0:T(8,128)(2,1)} %copy.23), calls=%async_computation.1 | async-start | bytes 5505024 | tf_op jit(solution)/shard_map/all_to_all | solution.py:36
Sparse Core Ops, SparseCore 0:
  122.1 121.5 all-gather.2
  246.1 71.3 all-reduce.1
